TPU v7x, 32 devices: a whole 2x2x4 slice. The times are simulated.
32 devices in a mesh: groups: 2 (over y), cent: 4 (over z), rows: 2 (over x), sub: 2 (over core).
Axes of the slice: x: 2, y: 2, z: 4, core: 2. Of those that a mesh axis runs over, the one named last changes fastest.
Arguments:
- embeddings: bfloat16 [4096, 768], P(('groups', 'cent', 'rows', 'sub')), parts along dimension 0, may hold values from -6 to 6
- coarse_lists: int32 [4096, 8], P(('groups', 'cent', 'rows', 'sub')), parts along dimension 0, may hold values from 0 to 127, all different within a row; in each aligned block of 128 rows (0 to 127, 128 to 255, ...) at most 16 rows name the same one
- coarse_table: bfloat16 [128, 768], replicated, may hold values from -6 to 6
- fine_table: bfloat16 [8192, 768], P(('cent', 'rows', 'sub')), may hold values from -6 to 6
Outputs:
- fine_out: bfloat16 [16384, 768], P(('groups', 'cent', 'rows', 'sub')), parts along dimension 0
- row_cost: float32 [4096], P(('groups', 'cent', 'rows', 'sub')), parts along dimension 0
- log_weights: float32 [256], P(('groups', 'cent', 'rows', 'sub')), parts along dimension 0
There are 2 independent parts, one for each index of `groups`. A program takes and returns all parts, laid end to end along the dimension named above; an argument that names none is the same for every part. Nothing has to cross between parts.
Inputs may be any that keep to these rules, and one draw needn't show every extreme that they name: `coarse_lists`: each row lists 8 different coarse clusters; among the rows of one device no cluster is listed by more than 16 rows, and in every draw some cluster is listed by exactly 16 rows of some device.
All inputs are finite; a program needn't handle non-finite values.
Results may differ from a plain program's by a relative error of at most 0.0024.
Values may be sent and summed in bfloat16 or wider, within the bound.
A program may use at most 64 MiB of HBM per device.

v0:
```python
import math

import jax
import jax.numpy as jnp
from jax import lax
from jax.sharding import PartitionSpec as P

FINE_PER = 64
TOP = 8
ITERS = 2


def body(embeddings, coarse_lists, coarse_table, fine_table):
    local_rows, model_width = embeddings.shape
    coarse_all = coarse_table.shape[0]
    clusters_dev = fine_table.shape[0] // FINE_PER
    cent_size = lax.axis_size("cent")
    rest_size = lax.axis_size(("rows", "sub"))
    devices = lax.axis_size(("cent", "rows", "sub"))
    rows_all = local_rows * devices
    most_rows = max(2, 2 * local_rows * TOP // coarse_all)
    factor = 1.0 / math.sqrt(model_width)
    slot_total = coarse_all * most_rows
    received = devices * most_rows
    coarse_norm = jnp.einsum(
        "kd,kd->k", coarse_table, coarse_table, preferred_element_type=jnp.float32
    )
    flat_ids = coarse_lists.reshape(-1)
    copies = flat_ids.shape[0]
    order_ids = jnp.argsort(flat_ids, stable=True)
    sorted_ids = flat_ids[order_ids]
    first_seen = jnp.searchsorted(sorted_ids, sorted_ids, side="left")
    sorted_position = jnp.arange(copies, dtype=jnp.int32) - first_seen
    position = jnp.zeros((copies,), jnp.int32).at[order_ids].set(sorted_position)
    slot_index = flat_ids * most_rows + position
    copy_rows = jnp.arange(copies, dtype=jnp.int32) // TOP
    source_row = jnp.full((slot_total,), -1, jnp.int32).at[slot_index].set(copy_rows)
    filled = source_row >= 0
    picked = embeddings[jnp.maximum(source_row, 0)]
    row_buffer = jnp.where(filled[:, None], picked, jnp.zeros_like(picked))
    row_buffer = row_buffer.reshape(cent_size, rest_size, clusters_dev, most_rows * model_width)
    log_weights = jnp.full((coarse_all,), -math.log(coarse_all), jnp.float32)
    fine_state = fine_table.astype(jnp.float32)
    row_cost = jnp.zeros((local_rows,), jnp.float32)
    got_rows = lax.all_to_all(
        lax.all_to_all(row_buffer, "cent", split_axis=0, concat_axis=3, tiled=True),
        ("rows", "sub"),
        split_axis=1,
        concat_axis=3,
        tiled=True,
    )
    for iteration in range(ITERS):
        coarse_dots = jnp.einsum(
            "rd,kd->rk", embeddings, coarse_table, preferred_element_type=jnp.float32
        )
        coarse_prob = jax.nn.softmax((coarse_dots - 0.5 * coarse_norm) * factor + log_weights, -1)
        masses = lax.psum(jnp.sum(coarse_prob, 0), ("cent", "rows", "sub"))
        listed = jnp.take_along_axis(coarse_prob, coarse_lists, 1)
        coarse_resp = (listed / jnp.sum(listed, -1, keepdims=True)).astype(jnp.bfloat16)
        resp_buffer = (
            jnp.zeros((slot_total,), jnp.bfloat16).at[slot_index].set(coarse_resp.reshape(-1))
        )
        resp_buffer = resp_buffer.reshape(cent_size, rest_size, clusters_dev, most_rows)
        got_resp = lax.all_to_all(
            lax.all_to_all(resp_buffer, "cent", split_axis=0, concat_axis=3, tiled=True),
            ("rows", "sub"),
            split_axis=1,
            concat_axis=3,
            tiled=True,
        )
        fine_bf = fine_state.astype(jnp.bfloat16)
        fine_norm = jnp.sum(jnp.square(fine_bf.astype(jnp.float32)), -1).reshape(
            clusters_dev, FINE_PER
        )
        slab_rows = got_rows.reshape(clusters_dev, received, model_width)
        slab_resp = got_resp.reshape(clusters_dev, received).astype(jnp.float32)
        centers = fine_bf.reshape(clusters_dev, FINE_PER, model_width)
        products = jnp.einsum(
            "cjd,csd->cjs", centers, slab_rows, preferred_element_type=jnp.float32
        )
        norm_term = fine_norm[:, :, None]
        shares = jax.nn.softmax((products - 0.5 * norm_term) * factor, 1)
        weight = (slab_resp[:, None, :] * shares).astype(jnp.bfloat16)
        fine_mass = jnp.sum(weight.astype(jnp.float32), 2).reshape(-1)
        stat_sums = jnp.einsum(
            "cjs,csd->cjd", weight, slab_rows, preferred_element_type=jnp.float32
        ).reshape(-1, model_width)
        if iteration == ITERS - 1:
            row_norm = jnp.einsum(
                "csd,csd->cs", slab_rows, slab_rows, preferred_element_type=jnp.float32
            )
            distance = row_norm[:, None, :] - 2.0 * products + norm_term
            slot_cost = slab_resp * jnp.sum(shares * distance, 1) / model_width
            slot_cost = slot_cost.reshape(1, 1, clusters_dev, rest_size, cent_size * most_rows)
            returned = lax.all_to_all(
                lax.all_to_all(slot_cost, "cent", split_axis=4, concat_axis=0, tiled=True),
                ("rows", "sub"),
                split_axis=3,
                concat_axis=1,
                tiled=True,
            )
            row_cost = jnp.sum(returned.reshape(-1)[slot_index].reshape(local_rows, TOP), -1)
        fine_state = (stat_sums + fine_state) / (fine_mass + 1.0)[:, None]
        log_weights = jnp.log((masses + 1.0) / (rows_all + coarse_all))
    device_index = lax.axis_index(("cent", "rows", "sub"))
    own_weights = lax.dynamic_slice_in_dim(log_weights, device_index * clusters_dev, clusters_dev)
    return (fine_state.astype(jnp.bfloat16), row_cost, own_weights)


def solution(mesh):
    return jax.shard_map(
        body,
        mesh=mesh,
        in_specs=(
            P(("groups", "cent", "rows", "sub"), None),
            P(("groups", "cent", "rows", "sub"), None),
            P(),
            P(("cent", "rows", "sub"), None),
        ),
        out_specs=(
            P(("groups", "cent", "rows", "sub"), None),
            P(("groups", "cent", "rows", "sub")),
            P(("groups", "cent", "rows", "sub")),
        ),
        check_vma=False,
    )
```

profile of v0, /device:TPU:0, one launch (start us, length us, event | category | flops | bytes accessed | tf_op | source)
XLA Modules:
  0.0 370.8 jit_solution(11523033594074501879)
XLA Ops:
  4.6 34.9 %psum.14 = f32[128]{0:T(128)S(1)} all-reduce(f32[128]{0:T(128)S(1)} %get-tuple-element.112), channel_id=1, replica_groups=mesh['groups'=2,'cent'=4,'rows'=2,'sub'=2] {'cent','rows','sub'}, use_global_device_ids=true, to_apply=%region_7.8 | all-reduce | flops 128 | bytes 1024 | tf_op jit(solution)/shard_map/psum | solution.py:57
  40.1 7.0 %gather_fusion.4 = f32[1024]{0:T(1024)S(1)} fusion(f32[128,128]{0,1:T(8,128)S(1)} %get-tuple-element.102, s32[1024]{0:T(1024)S(1)} %reshape.247), kind=kCustom, calls=%fused_computation.1.clone | custom fusion | bytes 16384 | tf_op jit(solution)/shard_map/jit(take_along_axis)/gather | solution.py:58
  47.3 7.0 %gather_fusion.5 = f32[1024]{0:T(1024)S(1)} fusion(f32[128,128]{0,1:T(8,128)S(1)} %get-tuple-element.113, s32[1024]{0:T(1024)S(1)} %reshape.247), kind=kCustom, calls=%fused_computation.2.clone | custom fusion | bytes 16384 | tf_op jit(solution)/shard_map/jit(take_along_axis)/gather | solution.py:58
  63.7 50.7 %while.25 = (s32[]{:T(128)}, u32[1024]{0:T(1024)S(1)}, u32[1024]{0:T(1024)S(1)}, s32[1024]{0:T(1024)S(1)}, s32[]{:T(128)}, /*index=5*/s32[]{:T(128)}, s32[]{}) while((s32[]{:T(128)}, u32[1024]{0:T(1024)S(1)}, u32[1024]{0:T(1024)S(1)}, s32[1024]{0:T(1024)S(1)}, s32[]{:T(128)}, /*index=5*/s32[]{:T(128)}, s32[]{}) %tuple.56), condition=%wide.region_2.3_spmd.clone, body=%wide.region_1.2_spmd.clone.sunk | while | flops 19460 | bytes 67685 | solution.py:32
  63.8 4.5 %gather_fusion = s32[1024]{0:T(1024)S(1)} fusion(s32[1024]{0:T(1024)S(1)} %get-tuple-element.172, u32[1024]{0:T(1024)S(1)} %broadcast_clamp_fusion.4), kind=kCustom, calls=%fused_computation.clone.clone.1 | custom fusion | bytes 12288 | tf_op jit(solution)/shard_map/jit(searchsorted)/jit(_searchsorted_scan_impl)/vmap(jit(_searchsorted_scan_impl))/while/body/eval_jaxpr/gather | solution.py:32
  68.4 4.5 %gather_fusion = s32[1024]{0:T(1024)S(1)} fusion(s32[1024]{0:T(1024)S(1)} %get-tuple-element.172, u32[1024]{0:T(1024)S(1)} %broadcast_clamp_fusion.4), kind=kCustom, calls=%fused_computation.clone.clone.1 | custom fusion | bytes 12288 | tf_op jit(solution)/shard_map/jit(searchsorted)/jit(_searchsorted_scan_impl)/vmap(jit(_searchsorted_scan_impl))/while/body/eval_jaxpr/gather | solution.py:32
  73.0 4.5 %gather_fusion = s32[1024]{0:T(1024)S(1)} fusion(s32[1024]{0:T(1024)S(1)} %get-tuple-element.172, u32[1024]{0:T(1024)S(1)} %broadcast_clamp_fusion.4), kind=kCustom, calls=%fused_computation.clone.clone.1 | custom fusion | bytes 12288 | tf_op jit(solution)/shard_map/jit(searchsorted)/jit(_searchsorted_scan_impl)/vmap(jit(_searchsorted_scan_impl))/while/body/eval_jaxpr/gather | solution.py:32
  77.6 4.5 %gather_fusion = s32[1024]{0:T(1024)S(1)} fusion(s32[1024]{0:T(1024)S(1)} %get-tuple-element.172, u32[1024]{0:T(1024)S(1)} %broadcast_clamp_fusion.4), kind=kCustom, calls=%fused_computation.clone.clone.1 | custom fusion | bytes 12288 | tf_op jit(solution)/shard_map/jit(searchsorted)/jit(_searchsorted_scan_impl)/vmap(jit(_searchsorted_scan_impl))/while/body/eval_jaxpr/gather | solution.py:32
  82.2 4.5 %gather_fusion = s32[1024]{0:T(1024)S(1)} fusion(s32[1024]{0:T(1024)S(1)} %get-tuple-element.172, u32[1024]{0:T(1024)S(1)} %broadcast_clamp_fusion.4), kind=kCustom, calls=%fused_computation.clone.clone.1 | custom fusion | bytes 12288 | tf_op jit(solution)/shard_map/jit(searchsorted)/jit(_searchsorted_scan_impl)/vmap(jit(_searchsorted_scan_impl))/while/body/eval_jaxpr/gather | solution.py:32
  86.8 4.5 %gather_fusion = s32[1024]{0:T(1024)S(1)} fusion(s32[1024]{0:T(1024)S(1)} %get-tuple-element.172, u32[1024]{0:T(1024)S(1)} %broadcast_clamp_fusion.4), kind=kCustom, calls=%fused_computation.clone.clone.1 | custom fusion | bytes 12288 | tf_op jit(solution)/shard_map/jit(searchsorted)/jit(_searchsorted_scan_impl)/vmap(jit(_searchsorted_scan_impl))/while/body/eval_jaxpr/gather | solution.py:32
  91.4 4.5 %gather_fusion = s32[1024]{0:T(1024)S(1)} fusion(s32[1024]{0:T(1024)S(1)} %get-tuple-element.172, u32[1024]{0:T(1024)S(1)} %broadcast_clamp_fusion.4), kind=kCustom, calls=%fused_computation.clone.clone.1 | custom fusion | bytes 12288 | tf_op jit(solution)/shard_map/jit(searchsorted)/jit(_searchsorted_scan_impl)/vmap(jit(_searchsorted_scan_impl))/while/body/eval_jaxpr/gather | solution.py:32
  96.1 4.5 %gather_fusion = s32[1024]{0:T(1024)S(1)} fusion(s32[1024]{0:T(1024)S(1)} %get-tuple-element.172, u32[1024]{0:T(1024)S(1)} %broadcast_clamp_fusion.4), kind=kCustom, calls=%fused_computation.clone.clone.1 | custom fusion | bytes 12288 | tf_op jit(solution)/shard_map/jit(searchsorted)/jit(_searchsorted_scan_impl)/vmap(jit(_searchsorted_scan_impl))/while/body/eval_jaxpr/gather | solution.py:32
  100.7 4.5 %gather_fusion = s32[1024]{0:T(1024)S(1)} fusion(s32[1024]{0:T(1024)S(1)} %get-tuple-element.172, u32[1024]{0:T(1024)S(1)} %broadcast_clamp_fusion.4), kind=kCustom, calls=%fused_computation.clone.clone.1 | custom fusion | bytes 12288 | tf_op jit(solution)/shard_map/jit(searchsorted)/jit(_searchsorted_scan_impl)/vmap(jit(_searchsorted_scan_impl))/while/body/eval_jaxpr/gather | solution.py:32
  105.3 4.5 %gather_fusion = s32[1024]{0:T(1024)S(1)} fusion(s32[1024]{0:T(1024)S(1)} %get-tuple-element.172, u32[1024]{0:T(1024)S(1)} %broadcast_clamp_fusion.4), kind=kCustom, calls=%fused_computation.clone.clone.1 | custom fusion | bytes 12288 | tf_op jit(solution)/shard_map/jit(searchsorted)/jit(_searchsorted_scan_impl)/vmap(jit(_searchsorted_scan_impl))/while/body/eval_jaxpr/gather | solution.py:32
  109.9 4.5 %gather_fusion = s32[1024]{0:T(1024)S(1)} fusion(s32[1024]{0:T(1024)S(1)} %get-tuple-element.172, u32[1024]{0:T(1024)S(1)} %broadcast_clamp_fusion.4), kind=kCustom, calls=%fused_computation.clone.clone.1 | custom fusion | bytes 12288 | tf_op jit(solution)/shard_map/jit(searchsorted)/jit(_searchsorted_scan_impl)/vmap(jit(_searchsorted_scan_impl))/while/body/eval_jaxpr/gather | solution.py:32
  118.8 7.6 %scatter_custom_fusion.2 = bf16[2048]{0:T(1024)(128)(2,1)S(1)} fusion(s32[1024]{0:T(1024)S(1)} %get-tuple-element.104, bf16[1024]{0:T(1024)(128)(2,1)S(1)} %reshape.213, bf16[]{:T(256)} %constant.93.clone.1), kind=kCustom, calls=%fused_computation.89 | custom fusion | bytes 4098 | tf_op jit(solution)/shard_map/scatter | solution.py:61
  135.0 9.4 %gather_fusion.2 = bf16[2048,768]{1,0:T(8,128)(2,1)} fusion(bf16[128,768]{1,0:T(8,128)(2,1)S(1)} %copy-done, s32[2048]{0:T(1024)S(1)} %maximum_clamp_fusion), kind=kCustom, calls=%fused_computation.4 | custom fusion | bytes 6299648 | tf_op jit(solution)/shard_map/gather | solution.py:39
  149.0 7.6 %scatter_custom_fusion.1 = bf16[2048]{0:T(1024)(128)(2,1)S(1)} fusion(s32[1024]{0:T(1024)S(1)} %get-tuple-element.104, bf16[1024]{0:T(1024)(128)(2,1)S(1)} %reshape.205, bf16[]{:T(256)} %constant.93.clone.1), kind=kCustom, calls=%fused_computation.91 | custom fusion | bytes 4098 | tf_op jit(solution)/shard_map/scatter | solution.py:61
  157.4 5.1 %all-to-all-start = ((bf16[4,2,256]{2,1,0:T(2,128)(2,1)}), bf16[4,2,256]{2,1,0:T(2,128)(2,1)S(1)}, u32[]{:S(2)}, u32[]{:S(2)}) async-start(bf16[4,2,256]{2,1,0:T(2,128)(2,1)} %reshape.268), calls=%async_computation | async-start | bytes 8192 | tf_op jit(solution)/shard_map/all_to_all | solution.py:65
  163.4 4.7 %all-to-all-done = bf16[4,2,256]{2,1,0:T(2,128)(2,1)S(1)} async-done(((bf16[4,2,256]{2,1,0:T(2,128)(2,1)}), bf16[4,2,256]{2,1,0:T(2,128)(2,1)S(1)}, u32[]{:S(2)}, u32[]{:S(2)}) %all-to-all-start) | async-done | bytes 4128 | tf_op jit(solution)/shard_map/all_to_all | solution.py:65
  179.6 70.0 %all-to-all-done.4 = bf16[4,4,8,12288]{3,2,1,0:T(8,128)(2,1)S(1)} async-done(((bf16[4,4,8,12288]{3,2,1,0:T(8,128)(2,1)}), bf16[4,4,8,12288]{3,2,1,0:T(8,128)(2,1)S(1)}, u32[]{:S(2)}, u32[]{:S(2)}) %all-to-all-start.4) | async-done | bytes 3145760 | tf_op jit(solution)/shard_map/all_to_all | solution.py:46
  261.8 57.5 %psum.15 = f32[128]{0:T(128)S(1)} all-reduce(f32[128]{0:T(128)S(1)} %get-tuple-element.101), channel_id=1, replica_groups=mesh['groups'=2,'cent'=4,'rows'=2,'sub'=2] {'cent','rows','sub'}, use_global_device_ids=true, to_apply=%region_26.28 | all-reduce | flops 128 | bytes 1024 | tf_op jit(solution)/shard_map/psum | solution.py:57
  324.3 5.6 %reshape.136 = bf16[8,256,768]{2,1,0:T(8,128)(2,1)S(1)} reshape(bf16[1,1,8,4,49152]{4,3,2,1,0:T(4,128)(2,1)} %copy.95) | data formatting | bytes 6291456 | tf_op jit(solution)/shard_map/reshape | solution.py:75
  364.0 6.1 %gather_fusion.3 = f32[1024]{0:T(1024)S(1)} fusion(f32[2048]{0:T(1024)S(1)} %reshape.141, s32[1024]{0:T(1024)S(1)} %get-tuple-element.103), kind=kCustom, calls=%fused_computation.5 | custom fusion | bytes 12288 | tf_op jit(solution)/shard_map/gather | solution.py:102
  (164 shorter events, 97.0 us)
Async XLA Ops:
  0.6 2.6 copy-start
  47.3 7.2 %copy-start.1 = (s32[128,8]{0,1:T(8,128)S(1)}, s32[128,8]{0,1:T(8,128)}, u32[]{:S(2)}) copy-start(s32[128,8]{0,1:T(8,128)} %param.9) | copy-start | bytes 12292
  127.2 30.2 %all-to-all-start.2 = ((bf16[4,2,256]{2,1,0:T(2,128)(2,1)}), bf16[4,2,256]{2,1,0:T(2,128)(2,1)S(1)}, u32[]{:S(2)}, u32[]{:S(2)}) async-start(bf16[4,2,256]{2,1,0:T(2,128)(2,1)} %reshape.272), calls=%async_computation.2 | async-start | bytes 8192 | tf_op jit(solution)/shard_map/all_to_all | solution.py:65
  157.4 10.6 %all-to-all-start = ((bf16[4,2,256]{2,1,0:T(2,128)(2,1)}), bf16[4,2,256]{2,1,0:T(2,128)(2,1)S(1)}, u32[]{:S(2)}, u32[]{:S(2)}) async-start(bf16[4,2,256]{2,1,0:T(2,128)(2,1)} %reshape.268), calls=%async_computation | async-start | bytes 8192 | tf_op jit(solution)/shard_map/all_to_all | solution.py:65
  168.0 7.0 %all-to-all-start.3 = ((bf16[4,2,256]{2,1,0:T(2,128)(2,1)}), bf16[4,2,256]{2,1,0:T(2,128)(2,1)S(1)}, u32[]{:S(2)}, u32[]{:S(2)}) async-start(bf16[4,2,256]{2,1,0:T(2,128)(2,1)} %reshape.274), calls=%async_computation.3 | async-start | bytes 8192 | tf_op jit(solution)/shard_map/all_to_all | solution.py:64
  175.0 74.6 %all-to-all-start.4 = ((bf16[4,4,8,12288]{3,2,1,0:T(8,128)(2,1)}), bf16[4,4,8,12288]{3,2,1,0:T(8,128)(2,1)S(1)}, u32[]{:S(2)}, u32[]{:S(2)}) async-start(bf16[4,4,8,12288]{3,2,1,0:T(8,128)(2,1)} %broadcast_select_fusion), calls=%async_computation.4 | async-start | bytes 6291456 | tf_op jit(solution)/shard_map/all_to_all | solution.py:46
  249.6 7.0 %all-to-all-start.1 = ((bf16[4,2,256]{2,1,0:T(2,128)(2,1)}), bf16[4,2,256]{2,1,0:T(2,128)(2,1)S(1)}, u32[]{:S(2)}, u32[]{:S(2)}) async-start(bf16[4,2,256]{2,1,0:T(2,128)(2,1)} %reshape.270), calls=%async_computation.1 | async-start | bytes 8192 | tf_op jit(solution)/shard_map/all_to_all | solution.py:64
  256.6 63.6 %all-to-all-start.5 = ((bf16[1,4,8,49152]{3,2,0,1:T(8,128)(2,1)}), bf16[1,4,8,49152]{3,2,0,1:T(8,128)(2,1)S(1)}, u32[]{:S(2)}, u32[]{:S(2)}) async-start(bf16[1,4,8,49152]{3,2,0,1:T(8,128)(2,1)} %bitcast.15), calls=%async_computation.5 | async-start | bytes 6291456 | tf_op jit(solution)/shard_map/all_to_all | solution.py:45
  345.0 8.8 %all-to-all-start.6 = ((f32[4,1,512]{2,1,0:T(1,128)}), f32[4,1,512]{2,1,0:T(1,128)S(1)}, u32[]{:S(2)}, u32[]{:S(2)}) async-start(f32[4,1,512]{2,1,0:T(1,128)} %reshape.276), calls=%async_computation.6 | async-start | bytes 16384 | tf_op jit(solution)/shard_map/all_to_all | solution.py:96
  356.0 7.0 %all-to-all-start.7 = ((f32[4,1,512]{2,1,0:T(1,128)}), f32[4,1,512]{2,1,0:T(1,128)S(1)}, u32[]{:S(2)}, u32[]{:S(2)}) async-start(f32[4,1,512]{2,1,0:T(1,128)} %reshape.278), calls=%async_computation.7 | async-start | bytes 16384 | tf_op jit(solution)/shard_map/all_to_all | solution.py:95
where the time goes:
time: 372 us; the launch traced here: 371 us
  local copies, waits for them, and re-layouts  134 us (36%)
  blocking collectives  92.4 us (25%)
  waiting for transfers between devices  80.9 us (22%)
  starting transfers between devices  28.7 us (8%)
  other arithmetic  23 us (6%)
  matrix products  10.7 us (3%)
    psum x2, blocking collectives, body(): masses = lax.psum(jnp.sum(coarse_prob, 0), ('cent', 'rows', 'sub'))  92.4 us
    all_to_all x1, waiting for transfers between devices, body(): lax.all_to_all(row_buffer, 'cent', split_axis=0, concat_axis=3, tiled=True)  70 us
    gather x11, local copies, waits for them, and re-layouts, body(): first_seen = jnp.searchsorted(sorted_ids, sorted_ids, side='left')  49.8 us
    scatter x2, local copies, waits for them, and re-layouts, body(): jnp.zeros((slot_total,), jnp.bfloat16).at[slot_index]  15.2 us
    gather x8, local copies, waits for them, and re-layouts, body(): listed = jnp.take_along_axis(coarse_prob, coarse_lists, 1)  14.5 us
    gather x2, local copies, waits for them, and re-layouts, body(): picked = embeddings[jnp.maximum(source_row, 0)]  13.6 us
    all_to_all x2, starting transfers between devices, body(): lax.all_to_all(resp_buffer, 'cent', split_axis=0, concat_axis=3, tiled=True)  8.3 us
  transfers between devices with their start and end apart: 8, of which 6 were waited for; matrix products, arithmetic and copies ran while one was open for 11% of the time, Pallas kernels for 0%

commit v1 on v0

--- a/solution.py
+++ b/solution.py
@@ -1,8 +1,12 @@
 import math
+
+import functools
 
 import jax
 import jax.numpy as jnp
 from jax import lax
+from jax.experimental import pallas as pl
+from jax.experimental.pallas import tpu as pltpu
 from jax.sharding import PartitionSpec as P
 
 FINE_PER = 64
@@ -10,7 +14,7 @@
 ITERS = 2
 
 
-def body(embeddings, coarse_lists, coarse_table, fine_table):
+def dispatch_body(embeddings, coarse_lists, coarse_table, fine_table):
     local_rows, model_width = embeddings.shape
     coarse_all = coarse_table.shape[0]
     clusters_dev = fine_table.shape[0] // FINE_PER
@@ -107,7 +111,441 @@
     return (fine_state.astype(jnp.bfloat16), row_cost, own_weights)
 
 
+GATHER_MAX = 8 * 1024 * 1024
+HALVES = 2
+MESH = pl.DeviceIdType.MESH
+
+
+def gather_kernel(
+    cent_size,
+    emb_ref,
+    lists_ref,
+    coarse_ref,
+    fine_ref,
+    fine_out_ref,
+    cost_out_ref,
+    weights_out_ref,
+    rows_all_ref,
+    lists_all_ref,
+    logits_ref,
+    prob_ref,
+    mass_ref,
+    fine_bf_ref,
+    state_ref,
+    half_norm_ref,
+    products_ref,
+    weight_ref,
+    stats_ref,
+    fine_mass_ref,
+    log_weights_ref,
+    resp_sum_ref,
+    cost_part_ref,
+    cost_got_ref,
+    row_send,
+    cross_send,
+    twin_send,
+    row_recv,
+    lists_send,
+    lists_recv,
+    cost_send,
+    cost_recv,
+):
+    local_rows, width = emb_ref.shape
+    coarse_all = coarse_ref.shape[0]
+    fine_dev = fine_ref.shape[0]
+    clusters_dev = fine_dev // FINE_PER
+    devices = 4 * cent_size
+    chips = 2 * cent_size
+    piece = local_rows // HALVES
+    chunk_rows = 2 * local_rows
+    factor = 1.0 / math.sqrt(width)
+    group = lax.axis_index("groups")
+    z = lax.axis_index("cent")
+    x = lax.axis_index("rows")
+    s = lax.axis_index("sub")
+    me = (z * 2 + x) * 2 + s
+    f32 = jnp.float32
+
+    def device(index):
+        return (group, index // 4, (index // 2) % 2, index % 2)
+
+    barrier = pltpu.get_barrier_semaphore()
+
+    def greet(step, carry):
+        other = lax.rem(me + step, devices)
+        pl.semaphore_signal(barrier, inc=1, device_id=device(other), device_id_type=MESH)
+        return carry
+
+    lax.fori_loop(1, devices, greet, 0)
+    pl.semaphore_wait(barrier, devices - 1)
+
+    def slot(zz, xx, ss, half):
+        return ((zz * 2 + xx) * 2 + ss) * HALVES + half
+
+    def copy_rows(src, index, sem, target):
+        return pltpu.make_async_remote_copy(
+            src_ref=src,
+            dst_ref=rows_all_ref.at[index],
+            send_sem=sem,
+            recv_sem=row_recv.at[index],
+            device_id=target,
+            device_id_type=MESH,
+        )
+
+    def to_right(src, zz, half):
+        return copy_rows(src, slot(zz, x, s, half), row_send.at[0, zz, half], (group, z + 1, x, s))
+
+    def to_left(src, zz, half):
+        return copy_rows(src, slot(zz, x, s, half), row_send.at[1, zz, half], (group, z - 1, x, s))
+
+    def to_cross(src, zz, half):
+        return copy_rows(src, slot(zz, x, s, half), cross_send.at[zz, half], (group, z, 1 - x, s))
+
+    def to_twin(src, zz, xx, half):
+        return copy_rows(
+            src, slot(zz, xx, s, half), twin_send.at[zz, xx, half], (group, z, x, 1 - s)
+        )
+
+    def held(zz, xx, half):
+        return rows_all_ref.at[slot(zz, xx, s, half)]
+
+    def wait_rows(index):
+        copy_rows(rows_all_ref.at[index], index, twin_send.at[0, 0, 0], (group, z, x, 1 - s)).wait_recv()
+
+    for half in range(HALVES):
+        mine = emb_ref.at[pl.ds(half * piece, piece)]
+
+        @pl.when(z + 1 < cent_size)
+        def _():
+            to_right(mine, z, half).start()
+
+        @pl.when(z >= 1)
+        def _():
+            to_left(mine, z, half).start()
+
+        to_cross(mine, z, half).start()
+        to_twin(mine, z, x, half).start()
+
+    lists = lists_ref[...].astype(f32)
+    lane = lax.broadcasted_iota(jnp.int32, (local_rows, 128), 1)
+    wide = jnp.zeros((local_rows, 128), f32)
+    for t in range(TOP):
+        wide = jnp.where(lane == t, lists[:, t : t + 1], wide)
+    lists_all_ref[me] = jnp.transpose(wide)[:TOP].astype(jnp.int32)
+
+    def copy_lists(owner, other):
+        return pltpu.make_async_remote_copy(
+            src_ref=lists_all_ref.at[owner],
+            dst_ref=lists_all_ref.at[owner],
+            send_sem=lists_send.at[other],
+            recv_sem=lists_recv.at[owner],
+            device_id=device(other),
+            device_id_type=MESH,
+        )
+
+    def send_lists(step, carry):
+        copy_lists(me, lax.rem(me + step, devices)).start()
+        return carry
+
+    lax.fori_loop(1, devices, send_lists, 0)
+
+    for half in range(HALVES):
+        rows_all_ref[slot(z, x, s, half)] = emb_ref[pl.ds(half * piece, piece), :]
+    own_wide = emb_ref[...].astype(f32)
+    row_norm = jnp.sum(own_wide * own_wide, axis=1, keepdims=True)
+    row_norm = jnp.transpose(jnp.broadcast_to(row_norm, (local_rows, 128)))[0:1, :]
+
+    coarse_wide = coarse_ref[...].astype(f32)
+    coarse_half = 0.5 * jnp.sum(coarse_wide * coarse_wide, axis=1, keepdims=True)
+    fine_bf_ref[...] = fine_ref[...]
+    mass_ref[...] = jnp.zeros_like(mass_ref)
+    log_weights_ref[...] = jnp.full(log_weights_ref.shape, -math.log(coarse_all), f32)
+
+    def begin_iteration():
+        fine_wide = fine_bf_ref[...].astype(f32)
+        half_norm_ref[...] = jnp.broadcast_to(
+            0.5 * jnp.sum(fine_wide * fine_wide, axis=1, keepdims=True), half_norm_ref.shape
+        )
+        stats_ref[...] = jnp.zeros_like(stats_ref)
+        fine_mass_ref[...] = jnp.zeros_like(fine_mass_ref)
+
+    begin_iteration()
+    dims = (((1,), (1,)), ((), ()))
+    ones = jnp.ones((chunk_rows, 128), jnp.bfloat16)
+
+    def visit(chip, last):
+        base = chip * (2 * HALVES)
+        rows = rows_all_ref[pl.ds(base, 2 * HALVES)].reshape(chunk_rows, width)
+        if last:
+            logits = logits_ref[chip]
+        else:
+            dots = lax.dot_general(coarse_ref[...], rows, dims, preferred_element_type=f32)
+            logits = (dots - coarse_half) * factor
+            logits_ref[chip] = logits
+        products_ref[...] = lax.dot_general(
+            fine_bf_ref[...], rows, dims, preferred_element_type=f32
+        )
+        logits = logits + log_weights_ref[:, 0:1]
+        raised = jnp.exp(logits - jnp.max(logits, axis=0, keepdims=True))
+        prob = raised * (1.0 / jnp.sum(raised, axis=0, keepdims=True))
+        mass_ref[...] += prob[:, :128] + prob[:, 128:]
+        cluster = lax.broadcasted_iota(jnp.int32, (coarse_all, local_rows), 0)
+        masks = []
+        for core in range(2):
+            named = lists_all_ref[chip * 2 + core]
+            mask = cluster == named[0:1, :]
+            for t in range(1, TOP):
+                mask = jnp.logical_or(mask, cluster == named[t : t + 1, :])
+            masks.append(jnp.where(mask, prob[:, core * local_rows : (core + 1) * local_rows], 0.0))
+        listed = jnp.concatenate(masks, axis=1)
+        resp = listed / jnp.sum(listed, axis=0, keepdims=True)
+        resp = resp.astype(jnp.bfloat16).astype(f32)
+        prob_ref[...] = resp
+        if last:
+            resp_sum_ref[chip] = jnp.sum(resp, axis=0, keepdims=True)
+        own = prob_ref[pl.ds(pl.multiple_of(me * clusters_dev, clusters_dev), clusters_dev), :]
+        cost = jnp.zeros((1, chunk_rows), f32)
+        for k in range(clusters_dev):
+            span = pl.ds(k * FINE_PER, FINE_PER)
+            norm = half_norm_ref[span, :]
+            norm = jnp.concatenate([norm, norm], axis=1)
+            score = (products_ref[span, :] - norm) * factor
+            score_max = jnp.max(score, axis=0, keepdims=True)
+            grown = jnp.exp(score - score_max)
+            share_scale = own[k : k + 1, :] / jnp.sum(grown, axis=0, keepdims=True)
+            weight_ref[span, :] = (grown * share_scale).astype(jnp.bfloat16)
+            if last:
+                cost = cost + share_scale * jnp.sum(grown * score, axis=0, keepdims=True)
+        weight = weight_ref[...]
+        stats_ref[...] += lax.dot_general(
+            weight, rows, (((1,), (0,)), ((), ())), preferred_element_type=f32
+        )
+        fine_mass_ref[...] += lax.dot_general(
+            weight, ones, (((1,), (0,)), ((), ())), preferred_element_type=f32
+        )
+        if last:
+            cost = cost * (-2.0 / (factor * width))
+            for core in range(2):
+                cost_part_ref[chip * 2 + core] = cost[:, core * local_rows : (core + 1) * local_rows]
+
+    def spread(step, carry):
+        for half in range(HALVES):
+            left_z, right_z = z - step - 1, z + step + 1
+
+            @pl.when(left_z >= 0)
+            def _():
+                wait_rows(slot(left_z, x, s, half))
+
+                @pl.when(z + 1 < cent_size)
+                def _():
+                    to_right(held(left_z, x, half), left_z, half).start()
+
+                to_cross(held(left_z, x, half), left_z, half).start()
+                to_twin(held(left_z, x, half), left_z, x, half).start()
+
+            @pl.when(right_z < cent_size)
+            def _():
+                wait_rows(slot(right_z, x, s, half))
+
+                @pl.when(z >= 1)
+                def _():
+                    to_left(held(right_z, x, half), right_z, half).start()
+
+                to_cross(held(right_z, x, half), right_z, half).start()
+                to_twin(held(right_z, x, half), right_z, x, half).start()
+
+        def crossed(side, carry):
+            zz = z - step + 2 * step * side
+            there = jnp.logical_and(zz >= 0, zz < cent_size)
+
+            @pl.when(jnp.logical_and(there, step + 1 > side))
+            def _():
+                for half in range(HALVES):
+                    wait_rows(slot(zz, 1 - x, s, half))
+                    to_twin(held(zz, 1 - x, half), zz, 1 - x, half).start()
+
+            return carry
+
+        def computed(turn, carry):
+            side = turn // 2
+            zz = z - step + 2 * step * side
+            xx = lax.rem(x + turn, 2)
+            there = jnp.logical_and(zz >= 0, zz < cent_size)
+
+            @pl.when(jnp.logical_and(there, step + 1 > side))
+            def _():
+                chip = zz * 2 + xx
+                for half in range(HALVES):
+                    wait_rows(slot(zz, xx, 1 - s, half))
+                for core in range(2):
+
+                    @pl.when(chip * 2 + core != me)
+                    def _():
+                        copy_lists(chip * 2 + core, lax.rem(me + 1, devices)).wait_recv()
+
+                visit(chip, False)
+
+            return carry
+
+        lax.fori_loop(0, 2, crossed, 0)
+        lax.fori_loop(0, 4, computed, 0)
+        return carry
+
+    lax.fori_loop(0, cent_size, spread, 0)
+
+    def new_state(previous):
+        scale = 1.0 / (fine_mass_ref[...] + 1.0)
+        scale = jnp.concatenate([scale] * (width // 128), axis=1)
+        return (stats_ref[...] + previous) * scale
+
+    def new_log_weights():
+        total = jnp.sum(mass_ref[...], axis=1, keepdims=True)
+        fresh = jnp.log((total + 1.0) / (devices * local_rows + coarse_all))
+        log_weights_ref[...] = jnp.broadcast_to(fresh, log_weights_ref.shape)
+        mass_ref[...] = jnp.zeros_like(mass_ref)
+
+    state = new_state(fine_ref[...].astype(f32))
+    state_ref[...] = state
+    fine_bf_ref[...] = state.astype(jnp.bfloat16)
+    new_log_weights()
+    begin_iteration()
+
+    def copy_cost(owner, other):
+        return pltpu.make_async_remote_copy(
+            src_ref=cost_part_ref.at[other],
+            dst_ref=cost_got_ref.at[owner],
+            send_sem=cost_send.at[other],
+            recv_sem=cost_recv.at[owner],
+            device_id=device(other),
+            device_id_type=MESH,
+        )
+
+    def second(step, carry):
+        chip = lax.rem(z * 2 + x + step, chips)
+        visit(chip, True)
+        for core in range(2):
+
+            @pl.when(chip * 2 + core != me)
+            def _():
+                copy_cost(me, chip * 2 + core).start()
+
+        return carry
+
+    lax.fori_loop(1, chips + 1, second, 0)
+
+    fine_out_ref[...] = new_state(state_ref[...]).astype(jnp.bfloat16)
+    new_log_weights()
+    own_weights = log_weights_ref[
+        pl.ds(pl.multiple_of(me * clusters_dev, clusters_dev), clusters_dev), :
+    ]
+    diagonal = lax.broadcasted_iota(jnp.int32, own_weights.shape, 0) == lax.broadcasted_iota(
+        jnp.int32, own_weights.shape, 1
+    )
+    own_weights = jnp.sum(jnp.where(diagonal, own_weights, 0.0), axis=0, keepdims=True)
+    weights_out_ref[...] = own_weights[:, :clusters_dev]
+
+    def drain(step, carry):
+        other = lax.rem(me + step, devices)
+        copy_lists(me, other).wait_send()
+        copy_cost(me, other).wait_send()
+        return carry
+
+    lax.fori_loop(1, devices, drain, 0)
+
+    def drain_rows(zz, carry):
+        for half in range(HALVES):
+
+            @pl.when(jnp.logical_and(z + 1 < cent_size, zz <= z))
+            def _():
+                to_right(held(zz, x, half), zz, half).wait_send()
+
+            @pl.when(jnp.logical_and(z >= 1, zz >= z))
+            def _():
+                to_left(held(zz, x, half), zz, half).wait_send()
+
+            to_cross(held(zz, x, half), zz, half).wait_send()
+            for xx in range(2):
+                to_twin(held(zz, xx, half), zz, xx, half).wait_send()
+        return carry
+
+    lax.fori_loop(0, cent_size, drain_rows, 0)
+
+    resp_sum = resp_sum_ref[z * 2 + x]
+    resp_sum = jnp.where(s == 0, resp_sum[:, :local_rows], resp_sum[:, local_rows:])
+    total = row_norm * resp_sum * (1.0 / width) + cost_part_ref[me]
+
+    def collect(step, total):
+        other = lax.rem(me + step, devices)
+        copy_cost(other, other).wait_recv()
+        return total + cost_got_ref[other]
+
+    cost_out_ref[...] = lax.fori_loop(1, devices, collect, total)
+
+
+def gather_body(cent_size, embeddings, coarse_lists, coarse_table, fine_table):
+    local_rows, width = embeddings.shape
+    coarse_all = coarse_table.shape[0]
+    fine_dev = fine_table.shape[0]
+    clusters_dev = fine_dev // FINE_PER
+    devices = 4 * cent_size
+    chips = 2 * cent_size
+    chunk = 2 * local_rows
+    f32, bf16 = jnp.float32, jnp.bfloat16
+    dma = pltpu.SemaphoreType.DMA
+    fine_out, row_cost, own_weights = pl.pallas_call(
+        functools.partial(gather_kernel, cent_size),
+        out_shape=(
+            jax.ShapeDtypeStruct((fine_dev, width), bf16),
+            jax.ShapeDtypeStruct((1, local_rows), f32),
+            jax.ShapeDtypeStruct((1, clusters_dev), f32),
+        ),
+        in_specs=[pl.BlockSpec(memory_space=pltpu.VMEM)] * 4,
+        out_specs=(pl.BlockSpec(memory_space=pltpu.VMEM),) * 3,
+        scratch_shapes=[
+            pltpu.VMEM((devices * HALVES, local_rows // HALVES, width), bf16),
+            pltpu.VMEM((devices, TOP, local_rows), jnp.int32),
+            pltpu.VMEM((chips, coarse_all, chunk), f32),
+            pltpu.VMEM((coarse_all, chunk), f32),
+            pltpu.VMEM((coarse_all, 128), f32),
+            pltpu.VMEM((fine_dev, width), bf16),
+            pltpu.VMEM((fine_dev, width), f32),
+            pltpu.VMEM((fine_dev, 128), f32),
+            pltpu.VMEM((fine_dev, chunk), f32),
+            pltpu.VMEM((fine_dev, chunk), bf16),
+            pltpu.VMEM((fine_dev, width), f32),
+            pltpu.VMEM((fine_dev, 128), f32),
+            pltpu.VMEM((coarse_all, 128), f32),
+            pltpu.VMEM((chips, 1, chunk), f32),
+            pltpu.VMEM((devices, 1, local_rows), f32),
+            pltpu.VMEM((devices, 1, local_rows), f32),
+            dma((2, cent_size, HALVES)),
+            dma((cent_size, HALVES)),
+            dma((cent_size, 2, HALVES)),
+            dma((devices * HALVES,)),
+            dma((devices,)),
+            dma((devices,)),
+            dma((devices,)),
+            dma((devices,)),
+        ],
+        compiler_params=pltpu.CompilerParams(
+            collective_id=0, has_side_effects=True, vmem_limit_bytes=40 * 1024 * 1024
+        ),
+    )(embeddings, coarse_lists, coarse_table, fine_table)
+    return fine_out, row_cost.reshape(-1), own_weights.reshape(-1)
+
+
 def solution(mesh):
+    sizes = dict(mesh.shape)
+
+    def body(embeddings, coarse_lists, coarse_table, fine_table):
+        devices = sizes["cent"] * sizes["rows"] * sizes["sub"]
+        gathered_bytes = 2 * devices * embeddings.size
+        fits = gathered_bytes <= GATHER_MAX and embeddings.shape[0] == 128
+        fits = fits and fine_table.shape[0] == 8 * FINE_PER
+        if sizes["rows"] == 2 and sizes["sub"] == 2 and fits:
+            return gather_body(sizes["cent"], embeddings, coarse_lists, coarse_table, fine_table)
+        return dispatch_body(embeddings, coarse_lists, coarse_table, fine_table)
+
     return jax.shard_map(
         body,
         mesh=mesh,

time: 372 us -> 49.1 us (0.13)
  local copies, waits for them, and re-layouts: 134 us -> 5.67 us
  blocking collectives: 92.4 us -> 0 us
  waiting for transfers between devices: 80.9 us -> 0 us
  Pallas kernels: 0 us -> 42.6 us
  starting transfers between devices: 28.7 us -> 0 us
  other arithmetic: 23 us -> 0 us
  matrix products: 10.7 us -> 0 us
    psum x2 -> x0, blocking collectives: 92.4 us -> none  [body(): masses = lax.psum(jnp.sum(coarse_prob, 0), ('cent', 'rows', 'sub'))]
    gather x23 -> x0, local copies, waits for them, and re-layouts: 88.5 us -> none  [the longest x11 49.8 us: body(): first_seen = jnp.searchsorted(sorted_ids, sorted_ids, side='left')]
    all_to_all x8 -> x0, waiting for transfers between devices: 80.9 us -> none  [the longest x1 70 us: body(): lax.all_to_all(row_buffer, 'cent', split_axis=0, concat_axis=3, tiled=True)]
    pallas_call x0 -> x1, Pallas kernels: none -> 42.6 us  [gather_body(): pl.pallas_call(functools.partial(gather_kernel, cent_size), out_shape=(ja...]
    all_to_all x8 -> x0, starting transfers between devices: 28.7 us -> none  [the longest x2 8.3 us: body(): lax.all_to_all(resp_buffer, 'cent', split_axis=0, concat_axis=3, tiled=True)]
    scatter x4 -> x0, local copies, waits for them, and re-layouts: 24 us -> none  [the longest x2 15.2 us: body(): jnp.zeros((slot_total,), jnp.bfloat16).at[slot_index]]
    reduce_sum x10 -> x0, other arithmetic: 7.7 us -> none  [the longest x2 3.41 us: body(): jnp.sum(jnp.square(fine_bf.astype(jnp.float32)), -1)]
    dot_general x4 -> x0, matrix products: 7.61 us -> none  [the longest x2 4.58 us: body(): jnp.einsum('cjs,csd->cjd', weight, slab_rows, preferred_element_type=jnp....]
  transfers between devices with their start and end apart: 8 -> 0, of which waited for: 6 -> 0; matrix products, arithmetic and copies ran while one was open for 11% -> 0% of each run, Pallas kernels for 0% -> 0%
where the time goes in v1:
time: 49.1 us; the launch traced here: 48.9 us
  Pallas kernels  42.6 us (87%)
  local copies, waits for them, and re-layouts  5.67 us (12%)
  between operations  0.65 us (1%)
    pallas_call x1, Pallas kernels, gather_body(): pl.pallas_call(functools.partial(gather_kernel, cent_size), out_shape=(ja...  42.6 us
    unnamed x10, local copies, waits for them, and re-layouts  5.67 us

profile of v1, /device:TPU:0, one launch (start us, length us, event | category | flops | bytes accessed | tf_op | source)
XLA Modules:
  0.0 48.9 jit_solution(13752429995029184810)
XLA Ops:
  0.6 0.8 %copy.7.lists_ref = s32[128,8]{1,0:T(8,128)S(1)} copy(s32[128,8]{0,1:T(8,128)} %param.5) | data formatting | bytes 8192 | tf_op args[1]
  1.4 0.0 copy-start
  1.4 1.1 %copy-done = bf16[512,768]{1,0:T(8,128)(2,1)S(1)} copy-done((bf16[512,768]{1,0:T(8,128)(2,1)S(1)}, bf16[512,768]{1,0:T(8,128)(2,1)}, u32[]{:S(2)}) %copy-start) | copy-done | bytes 786456
  2.6 0.0 copy-start.1
  2.6 0.9 %copy-done.1 = bf16[128,768]{1,0:T(8,128)(2,1)S(1)} copy-done((bf16[128,768]{1,0:T(8,128)(2,1)S(1)}, bf16[128,768]{1,0:T(8,128)(2,1)}, u32[]{:S(2)}) %copy-start.1) | copy-done | bytes 196632
  3.5 0.0 copy-start.2
  3.5 0.9 %copy-done.2 = bf16[128,768]{1,0:T(8,128)(2,1)S(1)} copy-done((bf16[128,768]{1,0:T(8,128)(2,1)S(1)}, bf16[128,768]{1,0:T(8,128)(2,1)}, u32[]{:S(2)}) %copy-start.2) | copy-done | bytes 196632
  4.4 42.6 %shard_map.67 = (bf16[512,768]{1,0:T(8,128)(2,1)S(1)}, f32[1,128]{1,0:T(1,128)S(1)}, f32[1,8]{1,0:T(1,128)S(1)}) custom-call(bf16[128,768]{1,0:T(8,128)(2,1)S(1)} %copy-done.1, s32[128,8]{1,0:T(8,128)S(1)} %copy.7.lists_ref, bf16[128,768]{1,0:T(8,128)(2,1)S(1)} %copy-done.2, bf16[512,768]{1,0:T(8,128)(2,1)S(1)} %copy-done), custom_call_target="tpu_custom_call" | custom-call | tf_op jit(solution)/shard_map/pallas_call | solution.py:495
  47.0 0.9 %copy.11 = bf16[512,768]{1,0:T(8,128)(2,1)} copy(bf16[512,768]{1,0:T(8,128)(2,1)S(1)} %get-tuple-element.12) | data formatting | bytes 1572864
  47.9 0.5 %copy.12 = f32[128]{0:T(128)} copy(f32[128]{0:T(128)S(1)} %bitcast.3) | data formatting | bytes 1024
  48.4 0.5 %copy.13 = f32[8]{0:T(128)} copy(f32[8]{0:T(128)S(1)} %bitcast.2) | data formatting | bytes 64
Async XLA Ops:
  1.4 1.1 %copy-start = (bf16[512,768]{1,0:T(8,128)(2,1)S(1)}, bf16[512,768]{1,0:T(8,128)(2,1)}, u32[]{:S(2)}) copy-start(bf16[512,768]{1,0:T(8,128)(2,1)} %fine_ref.1) | copy-start | bytes 2359300
  2.6 0.9 %copy-start.1 = (bf16[128,768]{1,0:T(8,128)(2,1)S(1)}, bf16[128,768]{1,0:T(8,128)(2,1)}, u32[]{:S(2)}) copy-start(bf16[128,768]{1,0:T(8,128)(2,1)} %emb_ref.1) | copy-start | bytes 589828
  3.5 0.9 %copy-start.2 = (bf16[128,768]{1,0:T(8,128)(2,1)S(1)}, bf16[128,768]{1,0:T(8,128)(2,1)}, u32[]{:S(2)}) copy-start(bf16[128,768]{1,0:T(8,128)(2,1)} %coarse_ref.1) | copy-start | bytes 589828

commit v2 on v1

v2 whole, which is shorter than its diff:
```python
import math

import functools

import jax
import jax.numpy as jnp
from jax import lax
from jax.experimental import pallas as pl
from jax.experimental.pallas import tpu as pltpu
from jax.sharding import PartitionSpec as P

FINE_PER = 64
TOP = 8
ITERS = 2


def dispatch_body(embeddings, coarse_lists, coarse_table, fine_table):
    local_rows, model_width = embeddings.shape
    coarse_all = coarse_table.shape[0]
    clusters_dev = fine_table.shape[0] // FINE_PER
    cent_size = lax.axis_size("cent")
    rest_size = lax.axis_size(("rows", "sub"))
    devices = lax.axis_size(("cent", "rows", "sub"))
    rows_all = local_rows * devices
    most_rows = max(2, 2 * local_rows * TOP // coarse_all)
    factor = 1.0 / math.sqrt(model_width)
    slot_total = coarse_all * most_rows
    received = devices * most_rows
    coarse_norm = jnp.einsum(
        "kd,kd->k", coarse_table, coarse_table, preferred_element_type=jnp.float32
    )
    flat_ids = coarse_lists.reshape(-1)
    copies = flat_ids.shape[0]
    order_ids = jnp.argsort(flat_ids, stable=True)
    sorted_ids = flat_ids[order_ids]
    first_seen = jnp.searchsorted(sorted_ids, sorted_ids, side="left")
    sorted_position = jnp.arange(copies, dtype=jnp.int32) - first_seen
    position = jnp.zeros((copies,), jnp.int32).at[order_ids].set(sorted_position)
    slot_index = flat_ids * most_rows + position
    copy_rows = jnp.arange(copies, dtype=jnp.int32) // TOP
    source_row = jnp.full((slot_total,), -1, jnp.int32).at[slot_index].set(copy_rows)
    filled = source_row >= 0
    picked = embeddings[jnp.maximum(source_row, 0)]
    row_buffer = jnp.where(filled[:, None], picked, jnp.zeros_like(picked))
    row_buffer = row_buffer.reshape(cent_size, rest_size, clusters_dev, most_rows * model_width)
    log_weights = jnp.full((coarse_all,), -math.log(coarse_all), jnp.float32)
    fine_state = fine_table.astype(jnp.float32)
    row_cost = jnp.zeros((local_rows,), jnp.float32)
    got_rows = lax.all_to_all(
        lax.all_to_all(row_buffer, "cent", split_axis=0, concat_axis=3, tiled=True),
        ("rows", "sub"),
        split_axis=1,
        concat_axis=3,
        tiled=True,
    )
    for iteration in range(ITERS):
        coarse_dots = jnp.einsum(
            "rd,kd->rk", embeddings, coarse_table, preferred_element_type=jnp.float32
        )
        coarse_prob = jax.nn.softmax((coarse_dots - 0.5 * coarse_norm) * factor + log_weights, -1)
        masses = lax.psum(jnp.sum(coarse_prob, 0), ("cent", "rows", "sub"))
        listed = jnp.take_along_axis(coarse_prob, coarse_lists, 1)
        coarse_resp = (listed / jnp.sum(listed, -1, keepdims=True)).astype(jnp.bfloat16)
        resp_buffer = (
            jnp.zeros((slot_total,), jnp.bfloat16).at[slot_index].set(coarse_resp.reshape(-1))
        )
        resp_buffer = resp_buffer.reshape(cent_size, rest_size, clusters_dev, most_rows)
        got_resp = lax.all_to_all(
            lax.all_to_all(resp_buffer, "cent", split_axis=0, concat_axis=3, tiled=True),
            ("rows", "sub"),
            split_axis=1,
            concat_axis=3,
            tiled=True,
        )
        fine_bf = fine_state.astype(jnp.bfloat16)
        fine_norm = jnp.sum(jnp.square(fine_bf.astype(jnp.float32)), -1).reshape(
            clusters_dev, FINE_PER
        )
        slab_rows = got_rows.reshape(clusters_dev, received, model_width)
        slab_resp = got_resp.reshape(clusters_dev, received).astype(jnp.float32)
        centers = fine_bf.reshape(clusters_dev, FINE_PER, model_width)
        products = jnp.einsum(
            "cjd,csd->cjs", centers, slab_rows, preferred_element_type=jnp.float32
        )
        norm_term = fine_norm[:, :, None]
        shares = jax.nn.softmax((products - 0.5 * norm_term) * factor, 1)
        weight = (slab_resp[:, None, :] * shares).astype(jnp.bfloat16)
        fine_mass = jnp.sum(weight.astype(jnp.float32), 2).reshape(-1)
        stat_sums = jnp.einsum(
            "cjs,csd->cjd", weight, slab_rows, preferred_element_type=jnp.float32
        ).reshape(-1, model_width)
        if iteration == ITERS - 1:
            row_norm = jnp.einsum(
                "csd,csd->cs", slab_rows, slab_rows, preferred_element_type=jnp.float32
            )
            distance = row_norm[:, None, :] - 2.0 * products + norm_term
            slot_cost = slab_resp * jnp.sum(shares * distance, 1) / model_width
            slot_cost = slot_cost.reshape(1, 1, clusters_dev, rest_size, cent_size * most_rows)
            returned = lax.all_to_all(
                lax.all_to_all(slot_cost, "cent", split_axis=4, concat_axis=0, tiled=True),
                ("rows", "sub"),
                split_axis=3,
                concat_axis=1,
                tiled=True,
            )
            row_cost = jnp.sum(returned.reshape(-1)[slot_index].reshape(local_rows, TOP), -1)
        fine_state = (stat_sums + fine_state) / (fine_mass + 1.0)[:, None]
        log_weights = jnp.log((masses + 1.0) / (rows_all + coarse_all))
    device_index = lax.axis_index(("cent", "rows", "sub"))
    own_weights = lax.dynamic_slice_in_dim(log_weights, device_index * clusters_dev, clusters_dev)
    return (fine_state.astype(jnp.bfloat16), row_cost, own_weights)


GATHER_MAX = 8 * 1024 * 1024
SPANS = ((0, 64), (64, 48), (112, 16))
LATE = len(SPANS) - 1
MESH = pl.DeviceIdType.MESH


def gather_kernel(
    cent_size,
    emb_ref,
    lists_ref,
    coarse_hbm_ref,
    fine_hbm_ref,
    fine_out_ref,
    cost_out_ref,
    weights_out_ref,
    coarse_ref,
    rows_all_ref,
    lists_all_ref,
    logits_ref,
    prob_ref,
    mask_ref,
    mass_ref,
    fine_bf_ref,
    half_norm_ref,
    products_ref,
    weight_ref,
    stats_ref,
    fine_mass_ref,
    log_weights_ref,
    cost_part_ref,
    cost_got_ref,
    load_sem,
    row_send,
    cross_send,
    twin_send,
    row_recv,
    lists_send,
    lists_recv,
    cost_send,
    cost_recv,
):
    local_rows, width = emb_ref.shape
    coarse_all = coarse_ref.shape[0]
    fine_dev = fine_bf_ref.shape[0]
    clusters_dev = fine_dev // FINE_PER
    devices = 4 * cent_size
    chips = 2 * cent_size
    chunk_rows = 2 * local_rows
    factor = 1.0 / math.sqrt(width)
    group = lax.axis_index("groups")
    z = lax.axis_index("cent")
    x = lax.axis_index("rows")
    s = lax.axis_index("sub")
    me = (z * 2 + x) * 2 + s
    f32 = jnp.float32

    def device(index):
        return (group, index // 4, (index // 2) % 2, index % 2)

    own_rows = rows_all_ref.at[pl.ds(pl.multiple_of(me * local_rows, local_rows), local_rows)]
    load_rows = pltpu.make_async_copy(emb_ref, own_rows, load_sem.at[0])
    load_lists = pltpu.make_async_copy(lists_ref, lists_all_ref.at[me], load_sem.at[1])
    load_coarse = pltpu.make_async_copy(coarse_hbm_ref, coarse_ref, load_sem.at[2])
    load_fine = pltpu.make_async_copy(fine_hbm_ref, fine_bf_ref, load_sem.at[3])
    load_rows.start()
    load_lists.start()
    load_coarse.start()
    load_fine.start()

    barrier = pltpu.get_barrier_semaphore()

    def greet(step, carry):
        other = lax.rem(me + step, devices)
        pl.semaphore_signal(barrier, inc=1, device_id=device(other), device_id_type=MESH)
        return carry

    lax.fori_loop(1, devices, greet, 0)
    pl.semaphore_wait(barrier, devices - 1)

    def copy_rows(zz, xx, ss, span, sem, target):
        owner = (zz * 2 + xx) * 2 + ss
        start, count = SPANS[span]
        place = rows_all_ref.at[pl.ds(pl.multiple_of(owner * local_rows + start, 16), count)]
        return pltpu.make_async_remote_copy(
            src_ref=place,
            dst_ref=place,
            send_sem=sem,
            recv_sem=row_recv.at[owner, span],
            device_id=target,
            device_id_type=MESH,
        )

    def to_right(zz, xx, span, way):
        return copy_rows(zz, xx, s, span, row_send.at[0, zz, way], (group, z + 1, x, s))

    def to_left(zz, xx, span, way):
        return copy_rows(zz, xx, s, span, row_send.at[1, zz, way], (group, z - 1, x, s))

    def to_cross(zz, span):
        return copy_rows(zz, x, s, span, cross_send.at[zz, span], (group, z, 1 - x, s))

    def to_twin(zz, xx, span):
        return copy_rows(zz, xx, s, span, twin_send.at[zz, xx, span], (group, z, x, 1 - s))

    def wait_rows(zz, xx, ss, span):
        copy_rows(zz, xx, ss, span, twin_send.at[0, 0, 0], (group, z, x, 1 - s)).wait_recv()

    def send_right(zz, xx, span, way):
        @pl.when(z + 1 < cent_size)
        def _():
            to_right(zz, xx, span, way).start()

    def send_left(zz, xx, span, way):
        @pl.when(z >= 1)
        def _():
            to_left(zz, xx, span, way).start()

    load_rows.wait()
    to_cross(z, LATE).start()
    for span in range(LATE):
        send_right(z, x, span, span)
        send_left(z, x, span, span)
        to_cross(z, span).start()
    send_right(z, x, LATE, LATE)
    send_left(z, x, LATE, LATE)
    for span in range(len(SPANS)):
        to_twin(z, x, span).start()
    load_lists.wait()

    def copy_lists(owner, other):
        return pltpu.make_async_remote_copy(
            src_ref=lists_all_ref.at[owner],
            dst_ref=lists_all_ref.at[owner],
            send_sem=lists_send.at[other],
            recv_sem=lists_recv.at[owner],
            device_id=device(other),
            device_id_type=MESH,
        )

    def send_lists(step, carry):
        copy_lists(me, lax.rem(me + step, devices)).start()
        return carry

    lax.fori_loop(1, devices, send_lists, 0)

    wait_rows(z, 1 - x, s, LATE)
    send_right(z, 1 - x, LATE, LATE + 1)
    send_left(z, 1 - x, LATE, LATE + 1)
    to_twin(z, 1 - x, LATE).start()

    load_coarse.wait()
    load_fine.wait()
    coarse_wide = coarse_ref[...].astype(f32)
    coarse_half = 0.5 * jnp.sum(coarse_wide * coarse_wide, axis=1, keepdims=True)
    mass_ref[...] = jnp.zeros_like(mass_ref)
    log_weights_ref[...] = jnp.full(log_weights_ref.shape, -math.log(coarse_all), f32)

    scale = factor * math.log2(math.e)

    def keep_norm(span, centers):
        wide = centers.astype(f32)
        norm = (0.5 * scale) * jnp.sum(wide * wide, axis=1, keepdims=True)
        half_norm_ref[span, :] = jnp.broadcast_to(norm, (FINE_PER, 128))

    spans = [pl.ds(k * FINE_PER, FINE_PER) for k in range(clusters_dev)]
    for span in spans:
        keep_norm(span, fine_bf_ref[span, :])
        stats_ref[span, :] = fine_bf_ref[span, :].astype(f32)
    fine_mass_ref[...] = jnp.zeros_like(fine_mass_ref)
    dims = (((1,), (1,)), ((), ()))
    plain = (((1,), (0,)), ((), ()))
    ones = jnp.ones((chunk_rows, 128), jnp.bfloat16)

    def rows_of(chip):
        return rows_all_ref[pl.ds(pl.multiple_of(chip * chunk_rows, chunk_rows), chunk_rows), :]

    def find_products(chip, buffer):
        products_ref[buffer] = lax.dot_general(
            fine_bf_ref[...], rows_of(chip), dims, preferred_element_type=f32
        )

    def find_logits(chip):
        dots = lax.dot_general(coarse_ref[...], rows_of(chip), dims, preferred_element_type=f32)
        logits_ref[chip] = (dots - coarse_half) * factor
        cluster = lax.broadcasted_iota(jnp.int32, (coarse_all, local_rows), 0)
        for core in range(2):
            named = lists_all_ref[chip * 2 + core]
            mask = cluster == named[0:1, :]
            for t in range(1, TOP):
                mask = jnp.logical_or(mask, cluster == named[t : t + 1, :])
            mask_ref[chip, :, core * local_rows : (core + 1) * local_rows] = mask.astype(f32)

    def find_resp(chip, buffer):
        logits = logits_ref[chip] + jnp.concatenate([log_weights_ref[...]] * 2, axis=1)
        raised = jnp.exp(logits - jnp.max(logits, axis=0, keepdims=True))
        prob = raised * (1.0 / jnp.sum(raised, axis=0, keepdims=True))
        mass_ref[...] += prob[:, :128] + prob[:, 128:]
        listed = mask_ref[chip] * prob
        prob_ref[buffer] = listed
        start = pl.multiple_of(me * clusters_dev, clusters_dev)
        own = prob_ref[buffer, pl.ds(start, clusters_dev), :]
        own = own / jnp.sum(listed, axis=0, keepdims=True)
        return own.astype(jnp.bfloat16).astype(f32)

    def find_weights(own, buffer, store, last):
        cost = jnp.zeros((1, chunk_rows), f32)
        for k, span in enumerate(spans):
            norm = half_norm_ref[span, :]
            score = products_ref[buffer, span, :] * scale - jnp.concatenate([norm, norm], axis=1)
            grown = jnp.exp2(score - jnp.max(score, axis=0, keepdims=True))
            share_scale = own[k : k + 1, :] / jnp.sum(grown, axis=0, keepdims=True)
            store(span, (grown * share_scale).astype(jnp.bfloat16))
            if last:
                cost = cost + share_scale * jnp.sum(grown * score, axis=0, keepdims=True)
        return cost

    def visit(chip):
        find_products(chip, 0)
        find_logits(chip)
        own = find_resp(chip, 0)

        def store(span, value):
            weight_ref[0, span, :] = value

        find_weights(own, 0, store, False)
        weight = weight_ref[0]
        stats_ref[...] += lax.dot_general(
            weight, rows_of(chip), plain, preferred_element_type=f32
        )
        fine_mass_ref[...] += lax.dot_general(weight, ones, plain, preferred_element_type=f32)

    def spread(step, carry):
        left_z, right_z = z - step - 1, z + step + 1
        for span in range(LATE + 2):
            xx = x if span <= LATE else 1 - x
            part = min(span, LATE)

            @pl.when(left_z >= 0)
            def _():
                wait_rows(left_z, xx, s, part)
                send_right(left_z, xx, part, span)
                if part < LATE:
                    to_cross(left_z, part).start()
                to_twin(left_z, xx, part).start()

            @pl.when(right_z < cent_size)
            def _():
                wait_rows(right_z, xx, s, part)
                send_left(right_z, xx, part, span)
                if part < LATE:
                    to_cross(right_z, part).start()
                to_twin(right_z, xx, part).start()

        def place(side):
            zz = z - step + 2 * step * side
            there = jnp.logical_and(zz >= 0, zz < cent_size)
            return zz, jnp.logical_and(there, step + 1 > side)

        def crossed(side, carry):
            zz, there = place(side)

            @pl.when(there)
            def _():
                for span in range(LATE):
                    wait_rows(zz, 1 - x, s, span)
                    to_twin(zz, 1 - x, span).start()

            return carry

        def computed(turn, carry):
            zz, there = place(lax.rem(turn, 2))
            xx = lax.rem(x + turn // 2, 2)

            @pl.when(turn == 2)
            def _():
                lax.fori_loop(0, 2, crossed, 0)

            @pl.when(there)
            def _():
                chip = zz * 2 + xx
                for span in range(len(SPANS)):
                    wait_rows(zz, xx, 1 - s, span)
                for core in range(2):

                    @pl.when(chip * 2 + core != me)
                    def _():
                        copy_lists(chip * 2 + core, lax.rem(me + 1, devices)).wait_recv()

                visit(chip)

            return carry

        lax.fori_loop(0, 4, computed, 0)
        return carry

    lax.fori_loop(0, cent_size, spread, 0)

    own_wide = own_rows[...].astype(f32)
    row_norm = jnp.sum(own_wide * own_wide, axis=1, keepdims=True)
    row_norm = jnp.transpose(jnp.broadcast_to(row_norm, (local_rows, 128)))[0:1, :]

    def new_log_weights():
        total = jnp.sum(mass_ref[...], axis=1, keepdims=True)
        fresh = jnp.log((total + 1.0) / (devices * local_rows + coarse_all))
        log_weights_ref[...] = jnp.broadcast_to(fresh, log_weights_ref.shape)
        mass_ref[...] = jnp.zeros_like(mass_ref)

    for span in spans:
        shrink = 1.0 / (fine_mass_ref[span, :] + 1.0)
        state = stats_ref[span, :] * jnp.concatenate([shrink] * (width // 128), axis=1)
        stats_ref[span, :] = state
        fine_bf_ref[span, :] = state.astype(jnp.bfloat16)
        keep_norm(span, fine_bf_ref[span, :])
    new_log_weights()

    def copy_cost(owner, other):
        return pltpu.make_async_remote_copy(
            src_ref=cost_part_ref.at[other],
            dst_ref=cost_got_ref.at[owner],
            send_sem=cost_send.at[other],
            recv_sem=cost_recv.at[owner],
            device_id=device(other),
            device_id_type=MESH,
        )

    def second(step, carry):
        pair = [lax.rem(z * 2 + x + 2 * step + 1 + i, chips) for i in range(2)]
        for i, chip in enumerate(pair):
            find_products(chip, i)
        for i, chip in enumerate(pair):
            own = find_resp(chip, i)

            def store(span, value):
                weight_ref[chip, span, :] = value

            cost = find_weights(own, i, store, True) * (-2.0 / (scale * width))
            for core in range(2):
                cost_part_ref[chip * 2 + core] = cost[:, core * local_rows : (core + 1) * local_rows]
        for chip in pair:
            for core in range(2):

                @pl.when(chip * 2 + core != me)
                def _():
                    copy_cost(me, chip * 2 + core).start()

        return carry

    lax.fori_loop(0, chips // 2, second, 0)

    weight = jnp.concatenate([weight_ref[chip] for chip in range(chips)], axis=1)
    all_ones = jnp.ones((chips * chunk_rows, 128), jnp.bfloat16)
    shrink = 1.0 / (lax.dot_general(weight, all_ones, plain, preferred_element_type=f32) + 1.0)
    wide_shrink = jnp.concatenate([shrink, shrink], axis=1)
    for start in range(0, width, 256):
        columns = pl.ds(start, 256)
        sums = lax.dot_general(
            weight, rows_all_ref[:, columns], plain, preferred_element_type=f32
        )
        state = (sums + stats_ref[:, columns]) * wide_shrink
        fine_out_ref[:, columns] = state.astype(jnp.bfloat16)
    listed = prob_ref[1]
    resp = listed / jnp.sum(listed, axis=0, keepdims=True)
    resp_sum = jnp.sum(resp.astype(jnp.bfloat16).astype(f32), axis=0, keepdims=True)
    new_log_weights()
    own_weights = log_weights_ref[
        pl.ds(pl.multiple_of(me * clusters_dev, clusters_dev), clusters_dev), :
    ]
    diagonal = lax.broadcasted_iota(jnp.int32, own_weights.shape, 0) == lax.broadcasted_iota(
        jnp.int32, own_weights.shape, 1
    )
    own_weights = jnp.sum(jnp.where(diagonal, own_weights, 0.0), axis=0, keepdims=True)
    weights_out_ref[...] = own_weights[:, :clusters_dev]

    def drain(step, carry):
        other = lax.rem(me + step, devices)
        copy_lists(me, other).wait_send()
        copy_cost(me, other).wait_send()
        return carry

    lax.fori_loop(1, devices, drain, 0)

    def drain_rows(zz, carry):
        for span in range(LATE + 2):
            xx = x if span <= LATE else 1 - x
            part = min(span, LATE)

            @pl.when(jnp.logical_and(z + 1 < cent_size, zz <= z))
            def _():
                to_right(zz, xx, part, span).wait_send()

            @pl.when(jnp.logical_and(z >= 1, zz >= z))
            def _():
                to_left(zz, xx, part, span).wait_send()

        for span in range(LATE):
            to_cross(zz, span).wait_send()
        for span in range(len(SPANS)):
            for xx in range(2):
                to_twin(zz, xx, span).wait_send()
        return carry

    to_cross(z, LATE).wait_send()
    lax.fori_loop(0, cent_size, drain_rows, 0)

    resp_sum = jnp.where(s == 0, resp_sum[:, :local_rows], resp_sum[:, local_rows:])
    total = row_norm * resp_sum * (1.0 / width) + cost_part_ref[me]

    def collect(step, total):
        other = lax.rem(me + step, devices)
        copy_cost(other, other).wait_recv()
        return total + cost_got_ref[other]

    cost_out_ref[...] = lax.fori_loop(1, devices, collect, total)


def write_kernel(fine_ref, cost_ref, weights_ref, fine_out, cost_out, weights_out, sem):
    pairs = ((fine_ref, fine_out), (cost_ref, cost_out), (weights_ref, weights_out))
    copies = [pltpu.make_async_copy(a, b, sem.at[i]) for i, (a, b) in enumerate(pairs)]
    for copy in copies:
        copy.start()
    for copy in copies:
        copy.wait()


def gather_body(cent_size, embeddings, coarse_lists, coarse_table, fine_table):
    local_rows, width = embeddings.shape
    coarse_all = coarse_table.shape[0]
    fine_dev = fine_table.shape[0]
    clusters_dev = fine_dev // FINE_PER
    devices = 4 * cent_size
    chips = 2 * cent_size
    chunk = 2 * local_rows
    f32, bf16 = jnp.float32, jnp.bfloat16
    dma = pltpu.SemaphoreType.DMA
    fine_out, row_cost, own_weights = pl.pallas_call(
        functools.partial(gather_kernel, cent_size),
        out_shape=(
            jax.ShapeDtypeStruct((fine_dev, width), bf16),
            jax.ShapeDtypeStruct((1, local_rows), f32),
            jax.ShapeDtypeStruct((1, clusters_dev), f32),
        ),
        in_specs=[pl.BlockSpec(memory_space=pltpu.HBM)] * 4,
        out_specs=(pl.BlockSpec(memory_space=pltpu.VMEM),) * 3,
        scratch_shapes=[
            pltpu.VMEM((coarse_all, width), bf16),
            pltpu.VMEM((devices * local_rows, width), bf16),
            pltpu.VMEM((devices, TOP, local_rows), jnp.int32),
            pltpu.VMEM((chips, coarse_all, chunk), f32),
            pltpu.VMEM((2, coarse_all, chunk), f32),
            pltpu.VMEM((chips, coarse_all, chunk), f32),
            pltpu.VMEM((coarse_all, 128), f32),
            pltpu.VMEM((fine_dev, width), bf16),
            pltpu.VMEM((fine_dev, 128), f32),
            pltpu.VMEM((2, fine_dev, chunk), f32),
            pltpu.VMEM((chips, fine_dev, chunk), bf16),
            pltpu.VMEM((fine_dev, width), f32),
            pltpu.VMEM((fine_dev, 128), f32),
            pltpu.VMEM((coarse_all, 128), f32),
            pltpu.VMEM((devices, 1, local_rows), f32),
            pltpu.VMEM((devices, 1, local_rows), f32),
            dma((4,)),
            dma((2, cent_size, len(SPANS) + 1)),
            dma((cent_size, len(SPANS))),
            dma((cent_size, 2, len(SPANS))),
            dma((devices, len(SPANS))),
            dma((devices,)),
            dma((devices,)),
            dma((devices,)),
            dma((devices,)),
        ],
        compiler_params=pltpu.CompilerParams(
            collective_id=0, has_side_effects=True, vmem_limit_bytes=60 * 1024 * 1024
        ),
    )(embeddings, coarse_lists.T, coarse_table, fine_table)
    results = (fine_out, row_cost, own_weights)
    fine_out, row_cost, own_weights = pl.pallas_call(
        write_kernel,
        out_shape=tuple(jax.ShapeDtypeStruct(a.shape, a.dtype) for a in results),
        in_specs=[pl.BlockSpec(memory_space=pltpu.VMEM)] * 3,
        out_specs=(pl.BlockSpec(memory_space=pltpu.HBM),) * 3,
        scratch_shapes=[dma((3,))],
    )(*results)
    return fine_out, row_cost.reshape(-1), own_weights.reshape(-1)


def solution(mesh):
    sizes = dict(mesh.shape)

    def body(embeddings, coarse_lists, coarse_table, fine_table):
        devices = sizes["cent"] * sizes["rows"] * sizes["sub"]
        gathered_bytes = 2 * devices * embeddings.size
        fits = gathered_bytes <= GATHER_MAX and embeddings.shape[0] == 128
        fits = fits and fine_table.shape[0] == 8 * FINE_PER
        if sizes["rows"] == 2 and sizes["sub"] == 2 and fits:
            return gather_body(sizes["cent"], embeddings, coarse_lists, coarse_table, fine_table)
        return dispatch_body(embeddings, coarse_lists, coarse_table, fine_table)

    return jax.shard_map(
        body,
        mesh=mesh,
        in_specs=(
            P(("groups", "cent", "rows", "sub"), None),
            P(("groups", "cent", "rows", "sub"), None),
            P(),
            P(("cent", "rows", "sub"), None),
        ),
        out_specs=(
            P(("groups", "cent", "rows", "sub"), None),
            P(("groups", "cent", "rows", "sub")),
            P(("groups", "cent", "rows", "sub")),
        ),
        check_vma=False,
    )
```

time: 49.1 us -> 43.8 us (0.89)
  local copies, waits for them, and re-layouts: 5.67 us -> 0 us
    unnamed x10 -> x0, local copies, waits for them, and re-layouts: 5.67 us -> none
    pallas_call x0 -> x1, Pallas kernels: none -> 2.05 us  [gather_body(): pl.pallas_call(write_kernel, out_shape=tuple((jax.ShapeDtypeStruct(a.shap...]
    pallas_call x1, Pallas kernels: 42.6 us -> 41 us  [gather_body(): pl.pallas_call(functools.partial(gather_kernel, cent_size), out_shape=(ja...]
where the time goes in v2:
time: 43.8 us; the launch traced here: 43.7 us
  Pallas kernels  43 us (98%)
  between operations  0.64 us (1%)
    pallas_call x1, Pallas kernels, gather_body(): pl.pallas_call(functools.partial(gather_kernel, cent_size), out_shape=(ja...  41 us
    pallas_call x1, Pallas kernels, gather_body(): pl.pallas_call(write_kernel, out_shape=tuple((jax.ShapeDtypeStruct(a.shap...  2.05 us

profile of v2, /device:TPU:0, one launch (start us, length us, event | category | flops | bytes accessed | tf_op | source)
XLA Modules:
  0.0 43.7 jit_solution(5055015186883407383)
XLA Ops:
  0.6 41.0 %shard_map.67 = (bf16[512,768]{1,0:T(8,128)(2,1)}, f32[1,128]{1,0:T(1,128)}, f32[1,8]{1,0:T(1,128)}) custom-call(bf16[128,768]{1,0:T(8,128)(2,1)} %emb_ref.1, s32[8,128]{1,0:T(8,128)} %bitcast.3, bf16[128,768]{1,0:T(8,128)(2,1)} %coarse_hbm_ref.1, bf16[512,768]{1,0:T(8,128)(2,1)} %fine_hbm_ref.1), custom_call_target="tpu_custom_call" | custom-call | tf_op jit(solution)/shard_map/pallas_call | solution.py:548
  41.6 2.0 %shard_map.68 = (bf16[512,768]{1,0:T(8,128)(2,1)}, f32[1,128]{1,0:T(1,128)}, f32[1,8]{1,0:T(1,128)}) custom-call(bf16[512,768]{1,0:T(8,128)(2,1)} %get-tuple-element.9.fine_ref, f32[1,128]{1,0:T(1,128)} %get-tuple-element.10.cost_ref, f32[1,8]{1,0:T(1,128)} %get-tuple-element.11.weights_ref), custom_call_target="tpu_custom_call" | custom-call | tf_op jit(solution)/shard_map/pallas_call | solution.py:589

commit v3 on v2

--- a/solution.py
+++ b/solution.py
@@ -112,6 +112,7 @@
 
 
 GATHER_MAX = 8 * 1024 * 1024
+PARTS = 4
 SPANS = ((0, 64), (64, 48), (112, 16))
 LATE = len(SPANS) - 1
 MESH = pl.DeviceIdType.MESH
@@ -256,11 +257,6 @@
 
     lax.fori_loop(1, devices, send_lists, 0)
 
-    wait_rows(z, 1 - x, s, LATE)
-    send_right(z, 1 - x, LATE, LATE + 1)
-    send_left(z, 1 - x, LATE, LATE + 1)
-    to_twin(z, 1 - x, LATE).start()
-
     load_coarse.wait()
     load_fine.wait()
     coarse_wide = coarse_ref[...].astype(f32)
@@ -343,12 +339,19 @@
         fine_mass_ref[...] += lax.dot_general(weight, ones, plain, preferred_element_type=f32)
 
     def spread(step, carry):
-        left_z, right_z = z - step - 1, z + step + 1
+        @pl.when(step == 1)
+        def _():
+            wait_rows(z, 1 - x, s, LATE)
+            send_right(z, 1 - x, LATE, LATE + 1)
+            send_left(z, 1 - x, LATE, LATE + 1)
+            to_twin(z, 1 - x, LATE).start()
+
+        left_z, right_z = z - step, z + step
         for span in range(LATE + 2):
             xx = x if span <= LATE else 1 - x
             part = min(span, LATE)
 
-            @pl.when(left_z >= 0)
+            @pl.when(jnp.logical_and(step >= 1, left_z >= 0))
             def _():
                 wait_rows(left_z, xx, s, part)
                 send_right(left_z, xx, part, span)
@@ -356,7 +359,7 @@
                     to_cross(left_z, part).start()
                 to_twin(left_z, xx, part).start()
 
-            @pl.when(right_z < cent_size)
+            @pl.when(jnp.logical_and(step >= 1, right_z < cent_size))
             def _():
                 wait_rows(right_z, xx, s, part)
                 send_left(right_z, xx, part, span)
@@ -364,31 +367,31 @@
                     to_cross(right_z, part).start()
                 to_twin(right_z, xx, part).start()
 
-        def place(side):
-            zz = z - step + 2 * step * side
+        def place(far, side):
+            zz = z - far + 2 * far * side
             there = jnp.logical_and(zz >= 0, zz < cent_size)
-            return zz, jnp.logical_and(there, step + 1 > side)
-
-        def crossed(side, carry):
-            zz, there = place(side)
-
-            @pl.when(there)
+            return zz, jnp.logical_and(there, far + 1 > side)
+
+        def crossed(side, far):
+            zz, there = place(far, side)
+
+            @pl.when(jnp.logical_and(there, far >= 0))
             def _():
                 for span in range(LATE):
                     wait_rows(zz, 1 - x, s, span)
                     to_twin(zz, 1 - x, span).start()
 
-            return carry
+            return far
+
+        lax.fori_loop(0, 2, crossed, step - 1)
 
         def computed(turn, carry):
-            zz, there = place(lax.rem(turn, 2))
-            xx = lax.rem(x + turn // 2, 2)
-
-            @pl.when(turn == 2)
-            def _():
-                lax.fori_loop(0, 2, crossed, 0)
-
-            @pl.when(there)
+            other = turn // 2
+            zz, there = place(step - other, lax.rem(turn, 2))
+            xx = lax.rem(x + other, 2)
+
+
+            @pl.when(jnp.logical_and(there, step >= other))
             def _():
                 chip = zz * 2 + xx
                 for span in range(len(SPANS)):
@@ -406,7 +409,7 @@
         lax.fori_loop(0, 4, computed, 0)
         return carry
 
-    lax.fori_loop(0, cent_size, spread, 0)
+    lax.fori_loop(0, cent_size + 1, spread, 0)
 
     own_wide = own_rows[...].astype(f32)
     row_norm = jnp.sum(own_wide * own_wide, axis=1, keepdims=True)
@@ -436,29 +439,26 @@
             device_id_type=MESH,
         )
 
-    def second(step, carry):
-        pair = [lax.rem(z * 2 + x + 2 * step + 1 + i, chips) for i in range(2)]
-        for i, chip in enumerate(pair):
-            find_products(chip, i)
-        for i, chip in enumerate(pair):
-            own = find_resp(chip, i)
-
-            def store(span, value):
-                weight_ref[chip, span, :] = value
-
-            cost = find_weights(own, i, store, True) * (-2.0 / (scale * width))
-            for core in range(2):
-                cost_part_ref[chip * 2 + core] = cost[:, core * local_rows : (core + 1) * local_rows]
-        for chip in pair:
-            for core in range(2):
-
-                @pl.when(chip * 2 + core != me)
-                def _():
-                    copy_cost(me, chip * 2 + core).start()
-
-        return carry
-
-    lax.fori_loop(0, chips // 2, second, 0)
+    order = [lax.rem(z * 2 + x + 1 + i, chips) for i in range(chips)]
+    find_products(order[0], 0)
+    find_products(order[1], 1)
+    for i, chip in enumerate(order):
+        if i % 2 == 0 and i + 2 < chips:
+            find_products(order[i + 2], (i + 2) % 4)
+            find_products(order[i + 3], (i + 3) % 4)
+        own = find_resp(chip, i % 2)
+
+        def store(span, value):
+            weight_ref[chip, span, :] = value
+
+        cost = find_weights(own, i % 4, store, True) * (-2.0 / (scale * width))
+        for core in range(2):
+            cost_part_ref[chip * 2 + core] = cost[:, core * local_rows : (core + 1) * local_rows]
+        if i + 1 < chips:
+            copy_cost(me, chip * 2).start()
+            copy_cost(me, chip * 2 + 1).start()
+        else:
+            copy_cost(me, chip * 2 + 1 - s).start()
 
     weight = jnp.concatenate([weight_ref[chip] for chip in range(chips)], axis=1)
     all_ones = jnp.ones((chips * chunk_rows, 128), jnp.bfloat16)
@@ -526,12 +526,21 @@
     cost_out_ref[...] = lax.fori_loop(1, devices, collect, total)
 
 
-def write_kernel(fine_ref, cost_ref, weights_ref, fine_out, cost_out, weights_out, sem):
-    pairs = ((fine_ref, fine_out), (cost_ref, cost_out), (weights_ref, weights_out))
-    copies = [pltpu.make_async_copy(a, b, sem.at[i]) for i, (a, b) in enumerate(pairs)]
-    for copy in copies:
+def write_kernel(fine_ref, cost_ref, weights_ref, fine_out, cost_out, weights_out, *rest):
+    fine_held, cost_held, weights_held, sem = rest
+    count = fine_ref.shape[0] // PARTS
+    hops = [(cost_ref, cost_held, cost_out), (weights_ref, weights_held, weights_out)]
+    for part in range(PARTS):
+        span = pl.ds(part * count, count)
+        hops.append((fine_ref.at[span], fine_held.at[span], fine_out.at[span]))
+    inward = [pltpu.make_async_copy(a, b, sem.at[0, i]) for i, (a, b, _) in enumerate(hops)]
+    outward = [pltpu.make_async_copy(b, c, sem.at[1, i]) for i, (_, b, c) in enumerate(hops)]
+    for copy in inward:
         copy.start()
-    for copy in copies:
+    for get, put in zip(inward, outward):
+        get.wait()
+        put.start()
+    for copy in outward:
         copy.wait()
 
 
@@ -564,7 +573,7 @@
             pltpu.VMEM((coarse_all, 128), f32),
             pltpu.VMEM((fine_dev, width), bf16),
             pltpu.VMEM((fine_dev, 128), f32),
-            pltpu.VMEM((2, fine_dev, chunk), f32),
+            pltpu.VMEM((4, fine_dev, chunk), f32),
             pltpu.VMEM((chips, fine_dev, chunk), bf16),
             pltpu.VMEM((fine_dev, width), f32),
             pltpu.VMEM((fine_dev, 128), f32),
@@ -589,9 +598,9 @@
     fine_out, row_cost, own_weights = pl.pallas_call(
         write_kernel,
         out_shape=tuple(jax.ShapeDtypeStruct(a.shape, a.dtype) for a in results),
-        in_specs=[pl.BlockSpec(memory_space=pltpu.VMEM)] * 3,
+        in_specs=[pl.BlockSpec(memory_space=pl.ANY)] * 3,
         out_specs=(pl.BlockSpec(memory_space=pltpu.HBM),) * 3,
-        scratch_shapes=[dma((3,))],
+        scratch_shapes=[pltpu.VMEM(a.shape, a.dtype) for a in results] + [dma((2, PARTS + 2))],
     )(*results)
     return fine_out, row_cost.reshape(-1), own_weights.reshape(-1)
 

time: 43.8 us -> 42.3 us (0.966)
  Pallas kernels: 43 us -> 41.5 us
    pallas_call x1, Pallas kernels: 41 us -> 39.5 us  [gather_body(): pl.pallas_call(functools.partial(gather_kernel, cent_size), out_shape=(ja...]
where the time goes in v3:
time: 42.3 us; the launch traced here: 42.1 us
  Pallas kernels  41.5 us (98%)
  between operations  0.64 us (2%)
    pallas_call x1, Pallas kernels, gather_body(): pl.pallas_call(functools.partial(gather_kernel, cent_size), out_shape=(ja...  39.5 us
    pallas_call x1, Pallas kernels, gather_body(): pl.pallas_call(write_kernel, out_shape=tuple((jax.ShapeDtypeStruct(a.shap...  2.01 us

profile of v3, /device:TPU:0, one launch (start us, length us, event | category | flops | bytes accessed | tf_op | source)
XLA Modules:
  0.0 42.1 jit_solution(11678726611124505691)
XLA Ops:
  0.6 39.5 %shard_map.67 = (bf16[512,768]{1,0:T(8,128)(2,1)}, f32[1,128]{1,0:T(1,128)}, f32[1,8]{1,0:T(1,128)}) custom-call(bf16[128,768]{1,0:T(8,128)(2,1)} %emb_ref.1, s32[8,128]{1,0:T(8,128)} %bitcast.3, bf16[128,768]{1,0:T(8,128)(2,1)} %coarse_hbm_ref.1, bf16[512,768]{1,0:T(8,128)(2,1)} %fine_hbm_ref.1), custom_call_target="tpu_custom_call" | custom-call | tf_op jit(solution)/shard_map/pallas_call | solution.py:557
  40.1 2.0 %shard_map.68 = (bf16[512,768]{1,0:T(8,128)(2,1)}, f32[1,128]{1,0:T(1,128)}, f32[1,8]{1,0:T(1,128)}) custom-call(bf16[512,768]{1,0:T(8,128)(2,1)} %get-tuple-element.9.fine_ref, f32[1,128]{1,0:T(1,128)} %get-tuple-element.10.cost_ref, f32[1,8]{1,0:T(1,128)} %get-tuple-element.11.weights_ref), custom_call_target="tpu_custom_call" | custom-call | tf_op jit(solution)/shard_map/pallas_call | solution.py:598

commit v4 on v3

--- a/solution.py
+++ b/solution.py
@@ -115,6 +115,7 @@
 PARTS = 4
 SPANS = ((0, 64), (64, 48), (112, 16))
 LATE = len(SPANS) - 1
+NAMES = LATE + 1
 MESH = pl.DeviceIdType.MESH
 
 
@@ -148,8 +149,6 @@
     cross_send,
     twin_send,
     row_recv,
-    lists_send,
-    lists_recv,
     cost_send,
     cost_recv,
 ):
@@ -193,8 +192,11 @@
 
     def copy_rows(zz, xx, ss, span, sem, target):
         owner = (zz * 2 + xx) * 2 + ss
-        start, count = SPANS[span]
-        place = rows_all_ref.at[pl.ds(pl.multiple_of(owner * local_rows + start, 16), count)]
+        if span == NAMES:
+            place = lists_all_ref.at[owner]
+        else:
+            start, count = SPANS[span]
+            place = rows_all_ref.at[pl.ds(pl.multiple_of(owner * local_rows + start, 16), count)]
         return pltpu.make_async_remote_copy(
             src_ref=place,
             dst_ref=place,
@@ -229,33 +231,21 @@
         def _():
             to_left(zz, xx, span, way).start()
 
+    ways = [(span, x, span) for span in range(NAMES + 1)]
+    ways += [(NAMES + 1, 1 - x, LATE), (NAMES + 2, 1 - x, NAMES)]
     load_rows.wait()
     to_cross(z, LATE).start()
+    load_lists.wait()
+    to_cross(z, NAMES).start()
     for span in range(LATE):
         send_right(z, x, span, span)
         send_left(z, x, span, span)
         to_cross(z, span).start()
-    send_right(z, x, LATE, LATE)
-    send_left(z, x, LATE, LATE)
-    for span in range(len(SPANS)):
+    for span in (LATE, NAMES):
+        send_right(z, x, span, span)
+        send_left(z, x, span, span)
+    for span in range(NAMES + 1):
         to_twin(z, x, span).start()
-    load_lists.wait()
-
-    def copy_lists(owner, other):
-        return pltpu.make_async_remote_copy(
-            src_ref=lists_all_ref.at[owner],
-            dst_ref=lists_all_ref.at[owner],
-            send_sem=lists_send.at[other],
-            recv_sem=lists_recv.at[owner],
-            device_id=device(other),
-            device_id_type=MESH,
-        )
-
-    def send_lists(step, carry):
-        copy_lists(me, lax.rem(me + step, devices)).start()
-        return carry
-
-    lax.fori_loop(1, devices, send_lists, 0)
 
     load_coarse.wait()
     load_fine.wait()
@@ -341,20 +331,19 @@
     def spread(step, carry):
         @pl.when(step == 1)
         def _():
-            wait_rows(z, 1 - x, s, LATE)
-            send_right(z, 1 - x, LATE, LATE + 1)
-            send_left(z, 1 - x, LATE, LATE + 1)
-            to_twin(z, 1 - x, LATE).start()
+            for way, xx, part in ways[NAMES + 1 :]:
+                wait_rows(z, xx, s, part)
+                send_right(z, xx, part, way)
+                send_left(z, xx, part, way)
+                to_twin(z, xx, part).start()
 
         left_z, right_z = z - step, z + step
-        for span in range(LATE + 2):
-            xx = x if span <= LATE else 1 - x
-            part = min(span, LATE)
+        for way, xx, part in ways:
 
             @pl.when(jnp.logical_and(step >= 1, left_z >= 0))
             def _():
                 wait_rows(left_z, xx, s, part)
-                send_right(left_z, xx, part, span)
+                send_right(left_z, xx, part, way)
                 if part < LATE:
                     to_cross(left_z, part).start()
                 to_twin(left_z, xx, part).start()
@@ -362,7 +351,7 @@
             @pl.when(jnp.logical_and(step >= 1, right_z < cent_size))
             def _():
                 wait_rows(right_z, xx, s, part)
-                send_left(right_z, xx, part, span)
+                send_left(right_z, xx, part, way)
                 if part < LATE:
                     to_cross(right_z, part).start()
                 to_twin(right_z, xx, part).start()
@@ -394,14 +383,8 @@
             @pl.when(jnp.logical_and(there, step >= other))
             def _():
                 chip = zz * 2 + xx
-                for span in range(len(SPANS)):
+                for span in range(NAMES + 1):
                     wait_rows(zz, xx, 1 - s, span)
-                for core in range(2):
-
-                    @pl.when(chip * 2 + core != me)
-                    def _():
-                        copy_lists(chip * 2 + core, lax.rem(me + 1, devices)).wait_recv()
-
                 visit(chip)
 
             return carry
@@ -486,33 +469,31 @@
 
     def drain(step, carry):
         other = lax.rem(me + step, devices)
-        copy_lists(me, other).wait_send()
         copy_cost(me, other).wait_send()
         return carry
 
     lax.fori_loop(1, devices, drain, 0)
 
     def drain_rows(zz, carry):
-        for span in range(LATE + 2):
-            xx = x if span <= LATE else 1 - x
-            part = min(span, LATE)
+        for way, xx, part in ways:
 
             @pl.when(jnp.logical_and(z + 1 < cent_size, zz <= z))
             def _():
-                to_right(zz, xx, part, span).wait_send()
+                to_right(zz, xx, part, way).wait_send()
 
             @pl.when(jnp.logical_and(z >= 1, zz >= z))
             def _():
-                to_left(zz, xx, part, span).wait_send()
+                to_left(zz, xx, part, way).wait_send()
 
         for span in range(LATE):
             to_cross(zz, span).wait_send()
-        for span in range(len(SPANS)):
+        for span in range(NAMES + 1):
             for xx in range(2):
                 to_twin(zz, xx, span).wait_send()
         return carry
 
     to_cross(z, LATE).wait_send()
+    to_cross(z, NAMES).wait_send()
     lax.fori_loop(0, cent_size, drain_rows, 0)
 
     resp_sum = jnp.where(s == 0, resp_sum[:, :local_rows], resp_sum[:, local_rows:])
@@ -581,12 +562,10 @@
             pltpu.VMEM((devices, 1, local_rows), f32),
             pltpu.VMEM((devices, 1, local_rows), f32),
             dma((4,)),
-            dma((2, cent_size, len(SPANS) + 1)),
-            dma((cent_size, len(SPANS))),
-            dma((cent_size, 2, len(SPANS))),
-            dma((devices, len(SPANS))),
-            dma((devices,)),
-            dma((devices,)),
+            dma((2, cent_size, NAMES + 3)),
+            dma((cent_size, NAMES + 1)),
+            dma((cent_size, 2, NAMES + 1)),
+            dma((devices, NAMES + 1)),
             dma((devices,)),
             dma((devices,)),
         ],

time: 42.3 us -> 41.8 us (0.988)
  Pallas kernels: 41.5 us -> 41 us
    pallas_call x1, Pallas kernels: 39.5 us -> 39 us  [gather_body(): pl.pallas_call(functools.partial(gather_kernel, cent_size), out_shape=(ja...]
where the time goes in v4:
time: 41.8 us; the launch traced here: 41.6 us
  Pallas kernels  41 us (98%)
  between operations  0.64 us (2%)
    pallas_call x1, Pallas kernels, gather_body(): pl.pallas_call(functools.partial(gather_kernel, cent_size), out_shape=(ja...  39 us
    pallas_call x1, Pallas kernels, gather_body(): pl.pallas_call(write_kernel, out_shape=tuple((jax.ShapeDtypeStruct(a.shap...  2.01 us

profile of v4, /device:TPU:0, one launch (start us, length us, event | category | flops | bytes accessed | tf_op | source)
XLA Modules:
  0.0 41.6 jit_solution(13692335366034994620)
XLA Ops:
  0.6 39.0 %shard_map.67 = (bf16[512,768]{1,0:T(8,128)(2,1)}, f32[1,128]{1,0:T(1,128)}, f32[1,8]{1,0:T(1,128)}) custom-call(bf16[128,768]{1,0:T(8,128)(2,1)} %emb_ref.1, s32[8,128]{1,0:T(8,128)} %bitcast.3, bf16[128,768]{1,0:T(8,128)(2,1)} %coarse_hbm_ref.1, bf16[512,768]{1,0:T(8,128)(2,1)} %fine_hbm_ref.1), custom_call_target="tpu_custom_call" | custom-call | tf_op jit(solution)/shard_map/pallas_call | solution.py:538
  39.6 2.0 %shard_map.68 = (bf16[512,768]{1,0:T(8,128)(2,1)}, f32[1,128]{1,0:T(1,128)}, f32[1,8]{1,0:T(1,128)}) custom-call(bf16[512,768]{1,0:T(8,128)(2,1)} %get-tuple-element.9.fine_ref, f32[1,128]{1,0:T(1,128)} %get-tuple-element.10.cost_ref, f32[1,8]{1,0:T(1,128)} %get-tuple-element.11.weights_ref), custom_call_target="tpu_custom_call" | custom-call | tf_op jit(solution)/shard_map/pallas_call | solution.py:577
